TPU v7x, 32 devices: a whole 2x2x4 slice. The times are simulated.
32 devices in a mesh: grp: 2 (over y), exp: 4 (over z), tp: 2 (over x), rep: 2 (over core).
Axes of the slice: x: 2, y: 2, z: 4, core: 2. Of those that a mesh axis runs over, the one named last changes fastest.
Arguments:
- tokens: bfloat16 [4096, 3584], P(('grp', 'exp', 'tp', 'rep')), parts along dimension 0, may hold values from -10 to 10
- routing: int32 [4096, 8], P(('grp', 'exp', 'tp', 'rep')), parts along dimension 0, may hold values from 0 to 255, as said below
- chosen: int32 [16], P('grp'), parts along dimension 0, may hold values from 0 to 3, as said below
- gate_matrix: bfloat16 [4, 3584, 1024], P('exp', None, 'tp'), may hold values from -0.09375 to 0.09375
- up_matrix: bfloat16 [4, 3584, 1024], P('exp', None, 'tp'), may hold values from -0.09375 to 0.09375
Outputs:
- hessians: float32 [16, 1024, 1024], P('grp', ('exp', 'rep'), 'tp'), parts along dimension 0
There are 2 independent parts, one for each index of `grp`. A program takes and returns all parts, laid end to end along the dimension named above; an argument that names none is the same for every part. Nothing has to cross between parts.
Inputs may be any that keep to these rules, and one draw needn't show every extreme that they name: `routing`: each row names 8 different experts, at most one of them below 4. Among the rows of one device, each expert below 4 is named by at least one and at most 6 rows; one expert below 4, the same for all devices of a group, is named by exactly 6 rows of every device. `chosen`: each expert below 4 appears exactly twice.
All inputs are finite; a program needn't handle non-finite values.
Results may differ from a plain program's by a relative error of at most 0.004.
Values may be sent and summed in bfloat16 or wider, within the bound.
A program may use at most 64 MiB of HBM per device.

v0:
```python
import jax
import jax.numpy as jnp
from jax import lax
from jax.sharding import PartitionSpec as P

FEATURE_HALF = 3584
ROW_CAPACITY = 6


def local(tokens, routing, chosen, gate_matrix, up_matrix):
    owners = lax.axis_size("exp")
    groups = lax.axis_size("tp")
    row_count = tokens.shape[0]
    slot_count = ROW_CAPACITY
    owner_indices = jnp.arange(owners, dtype=jnp.int32)
    member = jnp.sum(
        (routing[:, :, None] == owner_indices[None, None, :]).astype(jnp.int32), axis=1
    )
    local_counts = jnp.sum(member, axis=0).astype(jnp.float32)
    counts = lax.psum(local_counts, ("exp", "tp", "rep"))
    slot_rank = (jnp.cumsum(member, axis=0) - member).T
    slot_indices = jnp.arange(slot_count, dtype=jnp.int32)
    placing_mask = (slot_rank[:, None, :] == slot_indices[None, :, None]) & (
        member.T[:, None, :] > 0
    )
    picker = placing_mask.reshape(owners * slot_count, row_count).astype(jnp.bfloat16)
    packed = jnp.dot(picker, tokens, preferred_element_type=jnp.float32).astype(jnp.bfloat16)
    gate_local = gate_matrix[0]
    up_local = up_matrix[0]
    arrived = lax.all_to_all(
        packed.reshape(owners, slot_count, FEATURE_HALF),
        "exp",
        split_axis=0,
        concat_axis=0,
        tiled=True,
    )
    flat_rows = arrived.reshape(owners * slot_count, FEATURE_HALF)
    token_rows = lax.all_gather(flat_rows, "tp", axis=0, tiled=True)
    gate_out = jnp.dot(token_rows, gate_local, preferred_element_type=jnp.float32)
    up_out = jnp.dot(token_rows, up_local, preferred_element_type=jnp.float32)
    activated = (jax.nn.silu(gate_out) * up_out).astype(jnp.bfloat16)
    panel_width = activated.shape[1]
    full_width = panel_width * groups
    product = lax.dot_general(
        lax.all_gather(activated, "tp", axis=1, tiled=True),
        activated,
        (((0,), (0,)), ((), ())),
        preferred_element_type=jnp.float32,
    )
    hess_tile = product
    my_expert = lax.axis_index("exp")
    my_count = jnp.sum(jnp.where(owner_indices == my_expert, counts, 0.0))
    hess_tile = hess_tile * (2.0 / my_count)
    tile_rows = hess_tile.reshape(owners, full_width // owners, panel_width)
    summed = lax.psum_scatter(tile_rows, "rep", scatter_dimension=1, tiled=True)
    relocated = lax.all_to_all(summed, "exp", split_axis=0, concat_axis=0, tiled=True)
    return jnp.take(relocated, chosen, axis=0)


def solution(mesh):
    return jax.shard_map(
        local,
        mesh=mesh,
        in_specs=(
            P(("grp", "exp", "tp", "rep"), None),
            P(("grp", "exp", "tp", "rep"), None),
            P("grp"),
            P("exp", None, "tp"),
            P("exp", None, "tp"),
        ),
        out_specs=P("grp", ("exp", "rep"), "tp"),
        check_vma=False,
    )
```

profile of v0, /device:TPU:1, one launch (start us, length us, event | category | flops | bytes accessed | tf_op | source)
XLA Modules:
  0.0 115.5 jit_solution(9761766162891450428)
XLA Ops:
  6.5 0.0 copy-start
  6.5 0.9 convert_reduce_fusion
  7.5 0.1 copy.12
  7.6 0.2 reduce_window_sum.11
  7.8 0.1 copy.14
  7.9 0.1 eq.45
  8.0 0.0 copy-done
  8.0 0.3 convolution_convert_fusion
  8.3 0.8 reshape.22
  9.0 5.4 %all-to-all-start = ((bf16[4,6,3584]{2,1,0:T(8,128)(2,1)}), bf16[4,6,3584]{2,1,0:T(8,128)(2,1)S(1)}, u32[]{:S(2)}, u32[]{:S(2)}) async-start(bf16[4,6,3584]{2,1,0:T(8,128)(2,1)} %reshape.22), calls=%async_computation | async-start | bytes 458752 | tf_op jit(solution)/shard_map/all_to_all | solution.py:30
  14.5 0.0 reduce-scatter.2.cloned.1.call-start
  14.5 30.3 %psum.7 = f32[4]{0:T(128)S(1)} all-reduce(f32[4]{0:T(128)S(1)} %convert_element_type.16), channel_id=1, replica_groups=mesh['grp'=2,'exp'=4,'tp'=2,'rep'=2] {'exp','tp','rep'}, use_global_device_ids=true, to_apply=%region_3.0 | all-reduce | flops 4 | bytes 32 | tf_op jit(solution)/shard_map/psum | solution.py:20
  44.8 0.7 fusion.13
  46.2 0.0 all-to-all-done
  46.2 0.1 reshape.23
  46.3 4.9 %all_gather.6 = bf16[48,3584]{1,0:T(8,128)(2,1)S(1)} all-gather(bf16[24,3584]{1,0:T(8,128)(2,1)S(1)} %reshape.23), channel_id=1, replica_groups=mesh['grp'=2,'exp'=4,'tp'=2,'rep'=2] {'tp'}, dimensions={0}, use_global_device_ids=true | all-gather | bytes 516096 | tf_op jit(solution)/shard_map/all_gather | solution.py:38
  51.2 0.0 copy-start.1
  51.2 2.9 %fusion.2 = f32[48,512]{1,0:T(8,128)S(1)} fusion(bf16[48,3584]{1,0:T(8,128)(2,1)S(1)} %all_gather.6, bf16[1,3584,512]{2,1,0:T(8,128)(2,1)} %param.8), kind=kOutput, calls=%fused_computation.4 | convolution fusion | flops 176160768 | bytes 4112384 | tf_op jit(solution)/shard_map/dot_general | solution.py:39
  54.1 0.2 copy-done.1
  54.3 0.7 fusion.7
  55.1 3.6 %all_gather.7 = bf16[48,1024]{1,0:T(8,128)(2,1)S(1)} all-gather(bf16[48,512]{1,0:T(8,128)(2,1)S(1)} %fusion.7), channel_id=1, replica_groups=mesh['grp'=2,'exp'=4,'tp'=2,'rep'=2] {'tp'}, dimensions={1}, use_global_device_ids=true | all-gather | bytes 147456 | tf_op jit(solution)/shard_map/all_gather | solution.py:45
  58.7 1.8 %convolution_multiply_fusion = f32[1024,512]{1,0:T(8,128)} fusion(bf16[48,1024]{1,0:T(8,128)(2,1)S(1)} %all_gather.7, bf16[48,512]{1,0:T(8,128)(2,1)S(1)} %fusion.7, f32[]{:T(128)S(6)} %div.8), kind=kOutput, calls=%fused_computation.6 | convolution fusion | flops 50855936 | bytes 2244612 | tf_op jit(solution)/shard_map/dot_general | solution.py:44
  60.5 0.0 copy-start.2
  60.5 0.0 reduce-scatter.2.cloned.1.call-update
  60.5 12.8 %reduce-scatter.2.cloned.1.call-done = f32[4,128,512]{2,1,0:T(8,128)} async-done(((f32[4,256,512]{2,1,0:T(8,128)}), f32[4,128,512]{2,1,0:T(8,128)}) %reduce-scatter.2.cloned.1.call-update) | async-done | bytes 1048592 | tf_op jit(solution)/shard_map/reduce_scatter | solution.py:55
  73.3 4.7 %all-to-all-start.1 = ((f32[4,128,512]{2,1,0:T(8,128)}), f32[4,128,512]{2,1,0:T(8,128)S(1)}, u32[]{:S(2)}, u32[]{:S(2)}) async-start(f32[4,128,512]{2,1,0:T(8,128)} %reduce-scatter.2.cloned.1.call-done), calls=%async_computation.2 | async-start | bytes 2097152 | tf_op jit(solution)/shard_map/all_to_all | solution.py:56
  78.0 0.0 copy-done.2
  78.0 25.3 %all-to-all-done.1 = f32[4,128,512]{2,1,0:T(8,128)S(1)} async-done(((f32[4,128,512]{2,1,0:T(8,128)}), f32[4,128,512]{2,1,0:T(8,128)S(1)}, u32[]{:S(2)}, u32[]{:S(2)}) %all-to-all-start.1) | async-done | bytes 1048608 | tf_op jit(solution)/shard_map/all_to_all | solution.py:56
  103.3 2.0 %gather_fusion = f32[8,128,512]{2,1,0:T(8,128)} fusion(f32[4,128,512]{2,1,0:T(8,128)S(1)} %all-to-all-done.1, s32[1024]{0:T(1024)S(1)} %pad_clamp_fusion), kind=kCustom, calls=%fused_computation | custom fusion | bytes 4194336 | tf_op jit(solution)/shard_map/jit(_take)/gather | solution.py:57
  105.3 3.3 %broadcast_select_fusion = f32[8,128,512]{2,1,0:T(8,128)} fusion(f32[8,128,512]{2,1,0:T(8,128)} %gather_fusion, pred[8]{0:T(512)(128)(4,1)S(1)} %compare_and_fusion), kind=kLoop, calls=%fused_computation.9 | loop fusion | flops 524288 | bytes 4194312 | tf_op jit(solution)/shard_map/jit(_take)/select_n | solution.py:57
  (11 shorter events, 0.1 us)
Async XLA Ops:
  6.5 1.5 %copy-start = (bf16[128,3584]{1,0:T(8,128)(2,1)S(1)}, bf16[128,3584]{1,0:T(8,128)(2,1)}, u32[]{:S(2)}) copy-start(bf16[128,3584]{1,0:T(8,128)(2,1)} %param.5) | copy-start | bytes 2752516
  9.0 37.1 %all-to-all-start = ((bf16[4,6,3584]{2,1,0:T(8,128)(2,1)}), bf16[4,6,3584]{2,1,0:T(8,128)(2,1)S(1)}, u32[]{:S(2)}, u32[]{:S(2)}) async-start(bf16[4,6,3584]{2,1,0:T(8,128)(2,1)} %reshape.22), calls=%async_computation | async-start | bytes 458752 | tf_op jit(solution)/shard_map/all_to_all | solution.py:30
  14.5 58.8 %reduce-scatter.2.cloned.1.call-start = ((), (), s32[]{:S(2)}) async-start(), calls=%async_computation.3 | async-start | bytes 3145728 | tf_op jit(solution)/shard_map/reduce_scatter | solution.py:55
  51.2 3.1 %copy-start.1 = (bf16[1,3584,512]{2,1,0:T(8,128)(2,1)S(1)}, bf16[1,3584,512]{2,1,0:T(8,128)(2,1)}, u32[]{:S(2)}) copy-start(bf16[1,3584,512]{2,1,0:T(8,128)(2,1)} %param.9) | copy-start | bytes 11010052
  60.5 17.5 %copy-start.2 = (s32[8]{0:T(128)S(1)}, s32[8]{0:T(128)}, u32[]{:S(2)}) copy-start(s32[8]{0:T(128)} %param.7) | copy-start | bytes 100
  73.3 30.1 %all-to-all-start.1 = ((f32[4,128,512]{2,1,0:T(8,128)}), f32[4,128,512]{2,1,0:T(8,128)S(1)}, u32[]{:S(2)}, u32[]{:S(2)}) async-start(f32[4,128,512]{2,1,0:T(8,128)} %reduce-scatter.2.cloned.1.call-done), calls=%async_computation.2 | async-start | bytes 2097152 | tf_op jit(solution)/shard_map/all_to_all | solution.py:56
Sparse Core Ops, SparseCore 0:
  60.6 12.6 reduce-scatter.1
where the time goes:
time: 117 us; the launch traced here: 115 us
  blocking collectives  38.8 us (33%)
  waiting for transfers between devices  38.1 us (33%)
  between operations  14.2 us (12%)
  starting transfers between devices  10.1 us (9%)
  matrix products  5.7 us (5%)
  other arithmetic  5.11 us (4%)
  local copies, waits for them, and re-layouts  3.36 us (3%)
    psum x1, blocking collectives, local(): counts = lax.psum(local_counts, ('exp', 'tp', 'rep'))  30.3 us
    all_to_all x1, waiting for transfers between devices, local(): lax.all_to_all(summed, 'exp', split_axis=0, concat_axis=0, tiled=True)  25.3 us
    reduce_scatter x1, waiting for transfers between devices, local(): summed = lax.psum_scatter(tile_rows, 'rep', scatter_dimension=1, tiled=True)  12.8 us
    all_to_all x1, starting transfers between devices, local(): lax.all_to_all(packed.reshape(owners, slot_count, FEATURE_HALF), 'exp', s...  5.42 us
    all_gather x1, blocking collectives, local(): token_rows = lax.all_gather(flat_rows, 'tp', axis=0, tiled=True)  4.93 us
    all_to_all x1, starting transfers between devices, local(): lax.all_to_all(summed, 'exp', split_axis=0, concat_axis=0, tiled=True)  4.68 us
    all_gather x1, blocking collectives, local(): lax.all_gather(activated, 'tp', axis=1, tiled=True)  3.62 us
    select_n x2, other arithmetic, local(): return jnp.take(relocated, chosen, axis=0)  3.3 us
  transfers between devices with their start and end apart: 3, of which 2 were waited for; matrix products, arithmetic and copies ran while one was open for 1% of the time, Pallas kernels for 0%

commit v1 on v0

--- a/solution.py
+++ b/solution.py
@@ -1,10 +1,17 @@
+import functools
+
 import jax
 import jax.numpy as jnp
 from jax import lax
+from jax.experimental import pallas as pl
+from jax.experimental.pallas import tpu as pltpu
 from jax.sharding import PartitionSpec as P
 
 FEATURE_HALF = 3584
 ROW_CAPACITY = 6
+BLOCK = 16
+LANES = 128
+MESH = pl.DeviceIdType.MESH
 
 
 def local(tokens, routing, chosen, gate_matrix, up_matrix):
@@ -57,9 +64,263 @@
     return jnp.take(relocated, chosen, axis=0)
 
 
+def gather_kernel(owners, tokens_hbm, routing_ref, gate_hbm, up_hbm, cols_ref, rows_ref, counts_ref,
+                  tokens, gate, up, packed, arrived, half_mine, half_other,
+                  load_sem, z_send, z_recv, x_send, x_recv, c_send, c_recv,
+                  az_send, az_recv, ar_send, ar_recv, as_send, as_recv):
+    slots = ROW_CAPACITY
+    me, t, r = lax.axis_index("exp"), lax.axis_index("tp"), lax.axis_index("rep")
+    steps = STEP_ORDER
+    half = tokens.shape[1] // 2
+    panel = gate.shape[1]
+
+    loads = [
+        pltpu.make_async_copy(tokens_hbm, tokens, load_sem.at[0]),
+        pltpu.make_async_copy(gate_hbm.at[0], gate, load_sem.at[1]),
+        pltpu.make_async_copy(up_hbm.at[0], up, load_sem.at[2]),
+    ]
+    for load in loads:
+        load.start()
+
+    barrier = pltpu.get_barrier_semaphore()
+    peers = [{"exp": me ^ k, "tp": t, "rep": r} for k in steps]
+    peers += [{"exp": me, "tp": 1 - t, "rep": r}, {"exp": me, "tp": t, "rep": 1 - r}]
+    peers += [{"exp": me, "tp": 1 - t, "rep": 1 - r}]
+    for peer in peers:
+        pl.semaphore_signal(barrier, inc=1, device_id=peer, device_id_type=MESH)
+
+    routing = routing_ref[...]
+    count = routing.shape[1]
+    named = jnp.concatenate(
+        [jnp.sum((routing == j).astype(jnp.float32), axis=0, keepdims=True) for j in range(owners)]
+        + [jnp.zeros((8 - owners, count), jnp.float32)],
+        axis=0,
+    )
+    earlier = (
+        lax.broadcasted_iota(jnp.int32, (count, count), 0) < lax.broadcasted_iota(jnp.int32, (count, count), 1)
+    ).astype(jnp.float32).astype(jnp.bfloat16)
+    rank = jnp.dot(named.astype(jnp.bfloat16), earlier, preferred_element_type=jnp.float32)
+    local_counts = jnp.sum(named, axis=1, keepdims=True)
+    place = lax.broadcasted_iota(jnp.int32, (BLOCK, count), 0).astype(jnp.float32)
+    one = lax.broadcasted_iota(jnp.int32, (BLOCK, 1), 0)
+    first, second = [], []
+    count_rows = jnp.zeros((BLOCK, 1), jnp.float32)
+    for j in range(owners):
+        here = named[j : j + 1, :] > 0.5
+        first.append(jnp.where(here & (rank[j : j + 1, :] == place) & (place < slots), 1.0, 0.0))
+        second.append(
+            jnp.where(here & (rank[j : j + 1, :] == place - slots) & (place < 2 * slots), 1.0, 0.0)
+        )
+        count_rows = count_rows + jnp.where(one == 2 * slots + j, local_counts[j : j + 1, :], 0.0)
+    first = jnp.concatenate(first, axis=0).astype(jnp.bfloat16)
+    second = jnp.concatenate(second, axis=0).astype(jnp.bfloat16)
+    count_rows = jnp.concatenate([count_rows] * owners, axis=0)
+
+    loads[0].wait()
+    packed[...] = (
+        jnp.dot(first, tokens[:, :half], preferred_element_type=jnp.float32)
+        + jnp.dot(second, tokens[:, half:], preferred_element_type=jnp.float32)
+        + count_rows
+    ).astype(jnp.bfloat16).reshape(packed.shape)
+    arrived[t, me] = packed[me]
+
+    pl.semaphore_wait(barrier, len(peers))
+
+    def to_owner(k):
+        return pltpu.make_async_remote_copy(
+            src_ref=packed.at[me ^ k], dst_ref=arrived.at[t, me],
+            send_sem=z_send.at[k], recv_sem=z_recv.at[k],
+            device_id={"exp": me ^ k, "tp": t, "rep": r}, device_id_type=MESH,
+        )
+
+    def to_panel(k):
+        return pltpu.make_async_remote_copy(
+            src_ref=arrived.at[t, me ^ k], dst_ref=arrived.at[t, me ^ k],
+            send_sem=x_send.at[k], recv_sem=x_recv.at[k],
+            device_id={"exp": me, "tp": 1 - t, "rep": r}, device_id_type=MESH,
+        )
+
+    for k in steps:
+        to_owner(k).start()
+    to_panel(0).start()
+    for k in steps:
+        to_owner(k).wait_recv()
+        to_panel(k).start()
+    loads[1].wait()
+    loads[2].wait()
+    for k in (0,) + steps:
+        to_panel(k).wait_recv()
+
+    half_mine[...] = jnp.zeros_like(half_mine)
+    half_mine[0:owners, :] = jnp.sum(
+        arrived[:, :, 2 * slots : 2 * slots + owners, : half_mine.shape[1]].astype(jnp.float32), axis=(0, 1)
+    )
+    count_copy = pltpu.make_async_remote_copy(
+        src_ref=half_mine, dst_ref=half_other, send_sem=c_send, recv_sem=c_recv,
+        device_id={"exp": me, "tp": t, "rep": 1 - r}, device_id_type=MESH,
+    )
+    count_copy.start()
+
+    sources = arrived.shape[0] * arrived.shape[1]
+    total = sources * BLOCK
+    kept = sources * slots
+    out_row = lax.broadcasted_iota(jnp.int32, (kept, total), 0)
+    in_row = lax.broadcasted_iota(jnp.int32, (kept, total), 1)
+    source = in_row // BLOCK
+    slot = in_row - source * BLOCK
+    keep = ((slot < slots) & (out_row == source * slots + slot)).astype(jnp.float32).astype(jnp.bfloat16)
+    width = 256
+    for n in range(panel // width):
+        at = slice(n * width, (n + 1) * width)
+        x = arrived[...].reshape(total, half)
+
+        def both(w):
+            low = jnp.dot(x, w[:half, at], preferred_element_type=jnp.float32)
+            high = jnp.dot(x, w[half:, at], preferred_element_type=jnp.float32)
+            return low + pltpu.roll(high, total - slots, 0)
+
+        g = both(gate)
+        u = both(up)
+        a = ((g / (1.0 + jnp.exp(-g))) * u).astype(jnp.bfloat16)
+        cols_ref[me, r, :, at] = jnp.dot(keep, a, preferred_element_type=jnp.float32).astype(jnp.bfloat16)
+
+    def to_group(k):
+        return pltpu.make_async_remote_copy(
+            src_ref=cols_ref.at[me, r], dst_ref=cols_ref.at[me, r],
+            send_sem=az_send.at[k], recv_sem=az_recv.at[k],
+            device_id={"exp": me ^ k, "tp": t, "rep": r}, device_id_type=MESH,
+        )
+
+    def to_core(k):
+        return pltpu.make_async_remote_copy(
+            src_ref=cols_ref.at[me ^ k, r], dst_ref=cols_ref.at[me ^ k, r],
+            send_sem=ar_send.at[k], recv_sem=ar_recv.at[k],
+            device_id={"exp": me, "tp": t, "rep": 1 - r}, device_id_type=MESH,
+        )
+
+    rows_width = rows_ref.shape[3]
+    per_panel = panel // rows_width
+    in_panel = (me * 2) // per_panel
+    offset = me * 2 - in_panel * per_panel
+
+    def strip(core):
+        return pl.ds(pl.multiple_of((offset + core) * rows_width, rows_width), rows_width)
+
+    def to_rows(k, core, sender):
+        return pltpu.make_async_remote_copy(
+            src_ref=cols_ref.at[me ^ k, sender, :, strip(core)], dst_ref=rows_ref.at[me ^ k, sender],
+            send_sem=as_send.at[k, core], recv_sem=as_recv.at[k, sender],
+            device_id={"exp": me, "tp": 1 - t, "rep": core}, device_id_type=MESH,
+        )
+
+    def pass_on(k):
+        to_core(k).start()
+
+        @pl.when(t == in_panel)
+        def _():
+            to_rows(k, 0, r).start()
+            to_rows(k, 1, r).start()
+
+    for k in steps:
+        to_group(k).start()
+    pass_on(0)
+    for k in steps:
+        to_group(k).wait_recv()
+        pass_on(k)
+    for k in (0,) + steps:
+        to_core(k).wait_recv()
+
+    @pl.when(t == in_panel)
+    def _():
+        rows_ref[...] = cols_ref[:, :, :, strip(r)]
+        for k in (0,) + steps:
+            to_rows(k, 0, r).wait_send()
+            to_rows(k, 1, r).wait_send()
+
+    @pl.when(t != in_panel)
+    def _():
+        for k in (0,) + steps:
+            to_rows(k, r, 0).wait_recv()
+            to_rows(k, r, 1).wait_recv()
+
+    count_copy.wait()
+    counts_ref[...] = half_mine[...] + half_other[...]
+    for k in steps:
+        to_owner(k).wait_send()
+        to_group(k).wait_send()
+    for k in (0,) + steps:
+        to_panel(k).wait_send()
+        to_core(k).wait_send()
+
+
+def hessian_kernel(chosen_ref, cols_ref, rows_ref, counts_ref, out_hbm, tiles, sems):
+    copies = []
+    for s in range(out_hbm.shape[0]):
+        e = chosen_ref[s]
+        c = cols_ref[e].reshape(-1, cols_ref.shape[3])
+        w = rows_ref[e].reshape(-1, rows_ref.shape[3])
+        h = lax.dot_general(w, c, (((0,), (0,)), ((), ())), preferred_element_type=jnp.float32)
+        tiles[s] = h * (2.0 / counts_ref[pl.ds(e, 1), :])
+        copy = pltpu.make_async_copy(tiles.at[s], out_hbm.at[s], sems.at[s])
+        copy.start()
+        copies.append(copy)
+    for copy in copies:
+        copy.wait()
+
+
+STEP_ORDER = (2, 3, 1)
+
+
+def fused(owners, groups, tokens, routing, chosen, gate_matrix, up_matrix):
+    features, panel = gate_matrix.shape[1:]
+    kept = owners * groups * ROW_CAPACITY
+    rows_width = panel * groups // (owners * 2)
+    vmem = pl.BlockSpec(memory_space=pltpu.VMEM)
+    hbm = pl.BlockSpec(memory_space=pl.ANY)
+    dma = pltpu.SemaphoreType.DMA
+    cols, rows, counts = pl.pallas_call(
+        functools.partial(gather_kernel, owners),
+        out_shape=(
+            jax.ShapeDtypeStruct((owners, 2, kept, panel), jnp.bfloat16),
+            jax.ShapeDtypeStruct((owners, 2, kept, rows_width), jnp.bfloat16),
+            jax.ShapeDtypeStruct((8, panel), jnp.float32),
+        ),
+        in_specs=[hbm, vmem, hbm, hbm],
+        out_specs=(vmem, vmem, vmem),
+        scratch_shapes=[
+            pltpu.VMEM(tokens.shape, jnp.bfloat16),
+            pltpu.VMEM((features, panel), jnp.bfloat16),
+            pltpu.VMEM((features, panel), jnp.bfloat16),
+            pltpu.VMEM((owners, BLOCK, features // 2), jnp.bfloat16),
+            pltpu.VMEM((groups, owners, BLOCK, features // 2), jnp.bfloat16),
+            pltpu.VMEM((8, panel), jnp.float32),
+            pltpu.VMEM((8, panel), jnp.float32),
+            dma((3,)),
+            dma((owners,)), dma((owners,)), dma((owners,)), dma((owners,)),
+            dma, dma,
+            dma((owners,)), dma((owners,)), dma((owners,)), dma((owners,)),
+            dma((owners, 2)), dma((owners, 2)),
+        ],
+        compiler_params=pltpu.CompilerParams(
+            collective_id=0, has_side_effects=True, vmem_limit_bytes=40 * 1024 * 1024
+        ),
+    )(tokens, routing.T, gate_matrix, up_matrix)
+    out = (chosen.shape[0], rows_width, panel)
+    return pl.pallas_call(
+        hessian_kernel,
+        out_shape=jax.ShapeDtypeStruct(out, jnp.float32),
+        in_specs=[pl.BlockSpec(memory_space=pltpu.SMEM), vmem, vmem, vmem],
+        out_specs=hbm,
+        scratch_shapes=[pltpu.VMEM(out, jnp.float32), dma((out[0],))],
+        compiler_params=pltpu.CompilerParams(vmem_limit_bytes=24 * 1024 * 1024),
+    )(chosen, cols, rows, counts)
+
+
 def solution(mesh):
+    owners, groups, cores = mesh.shape["exp"], mesh.shape["tp"], mesh.shape["rep"]
+    small = owners == 4 and groups == 2 and cores == 2 and 2 * ROW_CAPACITY + owners <= BLOCK
     return jax.shard_map(
-        local,
+        functools.partial(fused, owners, groups) if small else local,
         mesh=mesh,
         in_specs=(
             P(("grp", "exp", "tp", "rep"), None),

time: 117 us -> 33.2 us (0.28)
  the two profiles are of different devices: /device:TPU:1 before, /device:TPU:0 now
where the time goes in v1:
time: 33.2 us; the launch traced here: 32.9 us
  Pallas kernels  26.9 us (81%)
  local copies, waits for them, and re-layouts  5.94 us (18%)
    pallas_call x1, Pallas kernels, fused(): pl.pallas_call(functools.partial(gather_kernel, owners), out_shape=(jax.S...  24.8 us
    unnamed x10, local copies, waits for them, and re-layouts  5.94 us
    pallas_call x1, Pallas kernels, fused(): pl.pallas_call(hessian_kernel, out_shape=jax.ShapeDtypeStruct(out, jnp.fl...  2.14 us

profile of v1, /device:TPU:0, one launch (start us, length us, event | category | flops | bytes accessed | tf_op | source)
XLA Modules:
  0.0 32.9 jit_solution(9183490694888774154)
XLA Ops:
  0.0 0.0 copy-start
  0.0 2.0 %copy-done = bf16[1,3584,512]{2,1,0:T(8,128)(2,1)S(1)} copy-done((bf16[1,3584,512]{2,1,0:T(8,128)(2,1)S(1)}, bf16[1,3584,512]{2,1,0:T(8,128)(2,1)}, u32[]{:S(2)}) %copy-start) | copy-done | bytes 3670040
  2.0 0.0 copy-start.1
  2.0 2.0 %copy-done.1 = bf16[1,3584,512]{2,1,0:T(8,128)(2,1)S(1)} copy-done((bf16[1,3584,512]{2,1,0:T(8,128)(2,1)S(1)}, bf16[1,3584,512]{2,1,0:T(8,128)(2,1)}, u32[]{:S(2)}) %copy-start.1) | copy-done | bytes 3670040
  4.1 0.0 copy-start.2
  4.1 1.2 %copy-done.2 = bf16[128,3584]{1,0:T(8,128)(2,1)S(1)} copy-done((bf16[128,3584]{1,0:T(8,128)(2,1)S(1)}, bf16[128,3584]{1,0:T(8,128)(2,1)}, u32[]{:S(2)}) %copy-start.2) | copy-done | bytes 917528
  5.3 0.0 copy-start.3
  5.3 0.7 %copy-done.3 = s32[128,8]{0,1:T(8,128)S(1)} copy-done((s32[128,8]{0,1:T(8,128)S(1)}, s32[128,8]{0,1:T(8,128)}, u32[]{:S(2)}) %copy-start.3) | copy-done | bytes 4120
  5.9 0.0 copy-start.4
  5.9 24.8 %shard_map.55 = (bf16[4,2,48,512]{3,2,1,0:T(8,128)(2,1)S(1)}, bf16[4,2,48,128]{3,2,1,0:T(8,128)(2,1)S(1)}, f32[8,512]{1,0:T(8,128)S(1)}) custom-call(bf16[128,3584]{1,0:T(8,128)(2,1)S(1)} %copy-done.2, s32[8,128]{1,0:T(8,128)S(1)} %bitcast.1, bf16[1,3584,512]{2,1,0:T(8,128)(2,1)S(1)} %copy-done, bf16[1,3584,512]{2,1,0:T(8,128)(2,1)S(1)} %copy-done.1), custom_call_target="tpu_custom_call" | custom-call | tf_op jit(solution)/shard_map/pallas_call | solution.py:281
  30.8 0.0 copy-done.4
  30.8 2.1 %shard_map.56 = f32[8,128,512]{2,1,0:T(8,128)} custom-call(s32[8]{0:T(128)S(1)} %copy-done.4, bf16[4,2,48,512]{3,2,1,0:T(8,128)(2,1)S(1)} %get-tuple-element.8.cols_ref, bf16[4,2,48,128]{3,2,1,0:T(8,128)(2,1)S(1)} %get-tuple-element.9.rows_ref, f32[8,512]{1,0:T(8,128)S(1)} %get-tuple-element.10.counts_ref), custom_call_target="tpu_custom_call" | custom-call | tf_op jit(solution)/shard_map/pallas_call | solution.py:309
Async XLA Ops:
  0.0 2.0 %copy-start = (bf16[1,3584,512]{2,1,0:T(8,128)(2,1)S(1)}, bf16[1,3584,512]{2,1,0:T(8,128)(2,1)}, u32[]{:S(2)}) copy-start(bf16[1,3584,512]{2,1,0:T(8,128)(2,1)} %gate_hbm.1) | copy-start | bytes 11010052
  2.0 2.0 %copy-start.1 = (bf16[1,3584,512]{2,1,0:T(8,128)(2,1)S(1)}, bf16[1,3584,512]{2,1,0:T(8,128)(2,1)}, u32[]{:S(2)}) copy-start(bf16[1,3584,512]{2,1,0:T(8,128)(2,1)} %up_hbm.1) | copy-start | bytes 11010052
  4.1 1.2 %copy-start.2 = (bf16[128,3584]{1,0:T(8,128)(2,1)S(1)}, bf16[128,3584]{1,0:T(8,128)(2,1)}, u32[]{:S(2)}) copy-start(bf16[128,3584]{1,0:T(8,128)(2,1)} %tokens_hbm.1) | copy-start | bytes 2752516
  5.3 0.7 %copy-start.3 = (s32[128,8]{0,1:T(8,128)S(1)}, s32[128,8]{0,1:T(8,128)}, u32[]{:S(2)}) copy-start(s32[128,8]{0,1:T(8,128)} %param.6) | copy-start | bytes 12292
  5.9 24.8 %copy-start.4 = (s32[8]{0:T(128)S(1)}, s32[8]{0:T(128)}, u32[]{:S(2)}) copy-start(s32[8]{0:T(128)} %chosen_ref.1) | copy-start | bytes 100

commit v2 on v0

--- a/solution.py
+++ b/solution.py
@@ -1,10 +1,21 @@
+import functools
+
 import jax
 import jax.numpy as jnp
 from jax import lax
+from jax.experimental import pallas as pl
+from jax.experimental.pallas import tpu as pltpu
 from jax.sharding import PartitionSpec as P
 
 FEATURE_HALF = 3584
 ROW_CAPACITY = 6
+BLOCK = 48
+CHUNK = 512
+WIDTH = 256
+EARLY = 32
+FAR = (2, 3)
+STEPS = (2, 3, 1)
+MESH = pl.DeviceIdType.MESH
 
 
 def local(tokens, routing, chosen, gate_matrix, up_matrix):
@@ -57,9 +68,274 @@
     return jnp.take(relocated, chosen, axis=0)
 
 
+def bits(mask):
+    return mask.astype(jnp.float32).astype(jnp.bfloat16)
+
+
+def hessian_kernel(owners, tokens_hbm, routing_hbm, gate_hbm, up_hbm, hess_ref,
+                   tokens, routing_ref, gate, up, packed, arrived, half_mine, half_other, cols, rows, chooser,
+                   load_sem, z_send, z_recv, f_send, f_recv, d_send, d_recv, c_send, c_recv,
+                   az_send, az_recv, ar_send, ar_recv, as_send, as_recv):
+    slots = ROW_CAPACITY
+    me, t, r = lax.axis_index("exp"), lax.axis_index("tp"), lax.axis_index("rep")
+    count, features = tokens.shape
+    chunks = features // CHUNK
+    pieces = gate.shape[1] // WIDTH
+    sources = arrived.shape[0] * owners
+    kept = sources * slots
+
+    def place(e, tp, rep):
+        return {"exp": e, "tp": tp, "rep": rep}
+
+    loads = [
+        pltpu.make_async_copy(routing_hbm, routing_ref, load_sem.at[0]),
+        pltpu.make_async_copy(tokens_hbm, tokens, load_sem.at[1]),
+        pltpu.make_async_copy(gate_hbm.at[0], gate, load_sem.at[2]),
+        pltpu.make_async_copy(up_hbm.at[0], up, load_sem.at[3]),
+    ]
+    for load in loads:
+        load.start()
+
+    barrier = pltpu.get_barrier_semaphore()
+    peers = [place(me ^ k, t ^ x, r ^ c) for k in range(owners) for x in (0, 1) for c in (0, 1)][1:]
+    for peer in peers:
+        pl.semaphore_signal(barrier, inc=1, device_id=peer, device_id_type=MESH)
+
+    loads[0].wait()
+    routing = routing_ref[...]
+    named = jnp.concatenate(
+        [jnp.sum((routing == j).astype(jnp.float32), axis=0, keepdims=True) for j in range(owners)]
+        + [jnp.zeros((8 - owners, count), jnp.float32)],
+        axis=0,
+    )
+    earlier = bits(
+        lax.broadcasted_iota(jnp.int32, (count, count), 0) < lax.broadcasted_iota(jnp.int32, (count, count), 1)
+    )
+    rank = jnp.dot(named.astype(jnp.bfloat16), earlier, preferred_element_type=jnp.float32)
+    local_counts = jnp.sum(named, axis=1, keepdims=True)
+    row = lax.broadcasted_iota(jnp.int32, (BLOCK, count), 0)
+    row_chunk = row // slots
+    row_slot = (row - row_chunk * slots).astype(jnp.float32)
+    one = lax.broadcasted_iota(jnp.int32, (BLOCK, 1), 0)
+    picker = []
+    count_rows = jnp.zeros((BLOCK, 1), jnp.float32)
+    for j in range(owners):
+        here = (named[j : j + 1, :] > 0.5) & (rank[j : j + 1, :] == row_slot)
+        picker.append(
+            jnp.concatenate([jnp.where(here & (row_chunk == c), 1.0, 0.0) for c in range(chunks)], axis=1)
+        )
+        count_rows = count_rows + jnp.where(one == chunks * slots + j, local_counts[j : j + 1, :], 0.0)
+    picker = jnp.concatenate(picker, axis=0).astype(jnp.bfloat16)
+    count_rows = jnp.concatenate([count_rows] * owners, axis=0)
+
+    loads[1].wait()
+    stacked = jnp.concatenate([tokens[:, c * CHUNK : (c + 1) * CHUNK] for c in range(chunks)], axis=0)
+    packed[...] = (
+        jnp.dot(picker, stacked, preferred_element_type=jnp.float32) + count_rows
+    ).astype(jnp.bfloat16).reshape(packed.shape)
+
+    pl.semaphore_wait(barrier, len(peers))
+
+    early, late = pl.ds(0, EARLY), pl.ds(EARLY, BLOCK - EARLY)
+
+    def remote(src, dst, send, recv, to):
+        return pltpu.make_async_remote_copy(
+            src_ref=src, dst_ref=dst, send_sem=send, recv_sem=recv, device_id=to, device_id_type=MESH
+        )
+
+    def to_owner(k):
+        return remote(packed.at[me ^ k, early], arrived.at[t, me, early], z_send.at[k], z_recv.at[k],
+                      place(me ^ k, t, r))
+
+    def forward(k):
+        here = arrived.at[t, me ^ k, early]
+        return remote(here, here, f_send.at[k], f_recv.at[k], place(me, 1 - t, r))
+
+    def direct(k, x, whole):
+        part = pl.ds(0, BLOCK) if whole else late
+        return remote(packed.at[me ^ k, part], arrived.at[t, me, part], d_send.at[k, x], d_recv.at[k, x],
+                      place(me ^ k, t ^ x, r))
+
+    directs = [(0, 1, True), (1, 0, True), (1, 1, True)] + [(k, x, False) for k in FAR for x in (0, 1)]
+    for k in FAR:
+        to_owner(k).start()
+    for d in directs:
+        direct(*d).start()
+    arrived[t, me] = packed[me]
+
+    total = sources * BLOCK
+    q = lax.broadcasted_iota(jnp.int32, (chunks * kept, 1), 0)
+    q_chunk = q // kept
+    q_row = q - q_chunk * kept
+    q_source = q_row // slots
+    target = q_source * BLOCK + q_chunk * slots + (q_row - q_source * slots)
+    chooser[...] = bits(lax.broadcasted_iota(jnp.int32, (chunks * kept, total), 1) == target)
+
+    for k in FAR:
+        to_owner(k).wait_recv()
+        forward(k).start()
+    for d in directs:
+        direct(*d).wait_recv()
+    for k in FAR:
+        forward(k).wait_recv()
+
+    half_mine[...] = jnp.zeros_like(half_mine)
+    half_mine[0:owners, :] = jnp.sum(
+        arrived[:, :, chunks * slots : chunks * slots + owners, :].astype(jnp.float32), axis=(0, 1)
+    )
+    count_copy = remote(half_mine, half_other, c_send, c_recv, place(me, t, 1 - r))
+    count_copy.start()
+
+    chosen_rows = jnp.dot(
+        chooser[...], arrived[...].reshape(total, CHUNK), preferred_element_type=jnp.float32
+    ).astype(jnp.bfloat16)
+    x = jnp.concatenate([chosen_rows[c * kept : (c + 1) * kept] for c in range(chunks)], axis=1)
+    loads[2].wait()
+    loads[3].wait()
+
+    def to_group(k, n):
+        here = cols.at[me, r, n]
+        return remote(here, here, az_send.at[k, n], az_recv.at[k, n], place(me ^ k, t, r))
+
+    def to_core(k, n):
+        here = cols.at[me ^ k, r, n]
+        return remote(here, here, ar_send.at[k, n], ar_recv.at[k, n], place(me, t, 1 - r))
+
+    strip_width = rows.shape[3]
+
+    def strip(core):
+        return pl.ds(pl.multiple_of(core * strip_width, strip_width), strip_width)
+
+    def to_strip(n, core):
+        return remote(cols.at[me, r, n, :, strip(core)], rows.at[me, r], as_send.at[n, core], as_recv.at[me, r],
+                      place(t * pieces + n, 1 - t, core))
+
+    def strip_arrival(e, core):
+        return remote(rows.at[e, core], rows.at[e, core], as_send.at[0, 0], as_recv.at[e, core], place(me, 1 - t, r))
+
+    for n in range(pieces):
+        at = slice(n * WIDTH, (n + 1) * WIDTH)
+        g = jnp.dot(x, gate[:, at], preferred_element_type=jnp.float32)
+        u = jnp.dot(x, up[:, at], preferred_element_type=jnp.float32)
+        cols[me, r, n] = ((g / (1.0 + jnp.exp(-g))) * u).astype(jnp.bfloat16)
+        for k in STEPS:
+            to_group(k, n).start()
+        for core in (0, 1):
+            to_strip(n, core).start()
+        to_core(0, n).start()
+
+    count_copy.wait()
+    half_mine[...] = 2.0 / jnp.maximum(half_mine[...] + half_other[...], 1.0)
+
+    in_panel = me // pieces
+
+    def hessian(k):
+        e = me ^ k
+        for n in range(pieces):
+            to_core(k, n).wait_recv()
+
+        @pl.when(t == in_panel)
+        def _():
+            rows[e] = cols[e, :, me - in_panel * pieces, :, strip(r)]
+
+        @pl.when(t != in_panel)
+        def _():
+            for core in (0, 1):
+                strip_arrival(e, core).wait_recv()
+
+        left = rows[e].reshape(2 * kept, strip_width)
+        scale = half_mine[pl.ds(e, 1), :]
+        for n in range(pieces):
+            right = jnp.concatenate([cols[e, 0, n], cols[e, 1, n]], axis=0)
+            h = lax.dot_general(left, right, (((0,), (0,)), ((), ())), preferred_element_type=jnp.float32)
+            at = slice(n * WIDTH, (n + 1) * WIDTH)
+            hess_ref[e, :, at] = h * scale[:, at]
+
+    for n in range(pieces):
+        for k in (1,) + FAR:
+            if n == pieces - 1 and k == FAR[0]:
+                hessian(0)
+            to_group(k, n).wait_recv()
+            to_core(k, n).start()
+    for k in (1,) + FAR:
+        hessian(k)
+
+    for k in FAR:
+        to_owner(k).wait_send()
+        forward(k).wait_send()
+    for d in directs:
+        direct(*d).wait_send()
+    for n in range(pieces):
+        for k in STEPS:
+            to_group(k, n).wait_send()
+        for k in (0,) + STEPS:
+            to_core(k, n).wait_send()
+        for core in (0, 1):
+            to_strip(n, core).wait_send()
+
+
+def order_kernel(chosen_ref, hess_ref, out_hbm, sems):
+    copies = [
+        pltpu.make_async_copy(hess_ref.at[chosen_ref[s]], out_hbm.at[s], sems.at[s]) for s in range(out_hbm.shape[0])
+    ]
+    for copy in copies:
+        copy.start()
+    for copy in copies:
+        copy.wait()
+
+
+def fused(owners, groups, tokens, routing, chosen, gate_matrix, up_matrix):
+    features, panel = gate_matrix.shape[1:]
+    kept = owners * groups * ROW_CAPACITY
+    chunks, pieces = features // CHUNK, panel // WIDTH
+    rows_width = panel * groups // (owners * 2)
+    vmem = pl.BlockSpec(memory_space=pltpu.VMEM)
+    hbm = pl.BlockSpec(memory_space=pltpu.HBM)
+    dma = pltpu.SemaphoreType.DMA
+    hess = pl.pallas_call(
+        functools.partial(hessian_kernel, owners),
+        out_shape=jax.ShapeDtypeStruct((owners, rows_width, panel), jnp.float32),
+        in_specs=[hbm, hbm, hbm, hbm],
+        out_specs=vmem,
+        scratch_shapes=[
+            pltpu.VMEM(tokens.shape, jnp.bfloat16),
+            pltpu.VMEM(routing.shape[::-1], jnp.int32),
+            pltpu.VMEM((features, panel), jnp.bfloat16),
+            pltpu.VMEM((features, panel), jnp.bfloat16),
+            pltpu.VMEM((owners, BLOCK, CHUNK), jnp.bfloat16),
+            pltpu.VMEM((groups, owners, BLOCK, CHUNK), jnp.bfloat16),
+            pltpu.VMEM((8, panel), jnp.float32),
+            pltpu.VMEM((8, panel), jnp.float32),
+            pltpu.VMEM((owners, 2, pieces, kept, WIDTH), jnp.bfloat16),
+            pltpu.VMEM((owners, 2, kept, rows_width), jnp.bfloat16),
+            pltpu.VMEM((chunks * kept, owners * groups * BLOCK), jnp.bfloat16),
+            dma((4,)),
+            dma((owners,)), dma((owners,)), dma((owners,)), dma((owners,)),
+            dma((owners, 2)), dma((owners, 2)),
+            dma, dma,
+            dma((owners, pieces)), dma((owners, pieces)), dma((owners, pieces)), dma((owners, pieces)),
+            dma((pieces, 2)), dma((owners, 2)),
+        ],
+        compiler_params=pltpu.CompilerParams(
+            collective_id=0, has_side_effects=True, vmem_limit_bytes=48 * 1024 * 1024
+        ),
+    )(*[pltpu.with_memory_space_constraint(a, pltpu.HBM) for a in (tokens, routing.T, gate_matrix, up_matrix)])
+    out = (chosen.shape[0], rows_width, panel)
+    return pl.pallas_call(
+        order_kernel,
+        out_shape=jax.ShapeDtypeStruct(out, jnp.float32),
+        in_specs=[pl.BlockSpec(memory_space=pltpu.SMEM), vmem],
+        out_specs=hbm,
+        scratch_shapes=[dma((out[0],))],
+        compiler_params=pltpu.CompilerParams(vmem_limit_bytes=24 * 1024 * 1024),
+    )(chosen, hess)
+
+
 def solution(mesh):
+    owners, groups, cores = mesh.shape["exp"], mesh.shape["tp"], mesh.shape["rep"]
+    small = owners == 4 and groups == 2 and cores == 2
     return jax.shard_map(
-        local,
+        functools.partial(fused, owners, groups) if small else local,
         mesh=mesh,
         in_specs=(
             P(("grp", "exp", "tp", "rep"), None),

time: 117 us -> 25.1 us (0.21); the launches traced: 115 us -> 25 us
  blocking collectives: 38.8 us -> 0 us
  waiting for transfers between devices: 38.1 us -> 0 us
  Pallas kernels: 0 us -> 25 us
  between operations: 14.2 us -> 0.02 us
  starting transfers between devices: 10.1 us -> 0 us
  matrix products: 5.7 us -> 0 us
  other arithmetic: 5.11 us -> 0 us
  local copies, waits for them, and re-layouts: 3.36 us -> 0.01 us
    psum x1 -> x0, blocking collectives: 30.3 us -> none  [local(): counts = lax.psum(local_counts, ('exp', 'tp', 'rep'))]
    all_to_all x2 -> x0, waiting for transfers between devices: 25.3 us -> none  [the longest x1 25.3 us: local(): lax.all_to_all(summed, 'exp', split_axis=0, concat_axis=0, tiled=True)]
    pallas_call x0 -> x2, Pallas kernels: none -> 25 us  [the longest x1 23 us: fused(): pl.pallas_call(functools.partial(hessian_kernel, owners), out_shape=jax.S...]
    reduce_scatter x1 -> x0, waiting for transfers between devices: 12.8 us -> none  [local(): summed = lax.psum_scatter(tile_rows, 'rep', scatter_dimension=1, tiled=True)]
    all_to_all x2 -> x0, starting transfers between devices: 10.1 us -> none  [the longest x1 5.42 us: local(): lax.all_to_all(packed.reshape(owners, slot_count, FEATURE_HALF), 'exp', s...]
    all_gather x2 -> x0, blocking collectives: 8.55 us -> none  [the longest x1 4.93 us: local(): token_rows = lax.all_gather(flat_rows, 'tp', axis=0, tiled=True)]
    dot_general x4 -> x0, matrix products: 5.7 us -> none  [the longest x1 2.91 us: local(): jnp.dot(token_rows, gate_local, preferred_element_type=jnp.float32)]
    select_n x2 -> x0, other arithmetic: 3.3 us -> none  [local(): return jnp.take(relocated, chosen, axis=0)]
  transfers between devices with their start and end apart: 3 -> 0, of which waited for: 2 -> 0; matrix products, arithmetic and copies ran while one was open for 1% -> 0% of each run, Pallas kernels for 0% -> 0%
where the time goes in v2:
time: 25.1 us; the launch traced here: 25 us
  Pallas kernels  25 us (100%)
    pallas_call x1, Pallas kernels, fused(): pl.pallas_call(functools.partial(hessian_kernel, owners), out_shape=jax.S...  23 us
    pallas_call x1, Pallas kernels, fused(): pl.pallas_call(order_kernel, out_shape=jax.ShapeDtypeStruct(out, jnp.floa...  1.92 us

profile of v2, /device:TPU:1, one launch (start us, length us, event | category | flops | bytes accessed | tf_op | source)
XLA Modules:
  0.0 25.0 jit_solution(8358123623685022393)
XLA Ops:
  0.0 0.0 copy-start
  0.0 23.0 %shard_map.55.hess_ref = f32[4,128,512]{2,1,0:T(8,128)S(1)} custom-call(bf16[128,3584]{1,0:T(8,128)(2,1)} %tokens_hbm.1, s32[8,128]{1,0:T(8,128)} %bitcast.1, bf16[1,3584,512]{2,1,0:T(8,128)(2,1)} %gate_hbm.1, bf16[1,3584,512]{2,1,0:T(8,128)(2,1)} %up_hbm.1), custom_call_target="tpu_custom_call" | custom-call | tf_op jit(solution)/shard_map/pallas_call | solution.py:295
  23.1 0.0 copy-done
  23.1 1.9 %shard_map.56 = f32[8,128,512]{2,1,0:T(8,128)} custom-call(s32[8]{0:T(128)S(1)} %copy-done, f32[4,128,512]{2,1,0:T(8,128)S(1)} %shard_map.55.hess_ref), custom_call_target="tpu_custom_call" | custom-call | tf_op jit(solution)/shard_map/pallas_call | solution.py:324
Async XLA Ops:
  0.0 23.1 %copy-start = (s32[8]{0:T(128)S(1)}, s32[8]{0:T(128)}, u32[]{:S(2)}) copy-start(s32[8]{0:T(128)} %chosen_ref.1) | copy-start | bytes 100

commit v3 on v2

--- a/solution.py
+++ b/solution.py
@@ -87,6 +87,12 @@
     def place(e, tp, rep):
         return {"exp": e, "tp": tp, "rep": rep}
 
+    barrier = pltpu.get_barrier_semaphore()
+    peers = [place(me ^ k, t ^ x, r ^ c) for k in (3, 2, 1) for x, c in ((0, 0), (1, 0), (1, 1))]
+    peers += [place(me, t ^ x, r ^ c) for x, c in ((1, 0), (1, 1), (0, 1))]
+    for peer in peers:
+        pl.semaphore_signal(barrier, inc=1, device_id=peer, device_id_type=MESH)
+
     loads = [
         pltpu.make_async_copy(routing_hbm, routing_ref, load_sem.at[0]),
         pltpu.make_async_copy(tokens_hbm, tokens, load_sem.at[1]),
@@ -95,11 +101,6 @@
     ]
     for load in loads:
         load.start()
-
-    barrier = pltpu.get_barrier_semaphore()
-    peers = [place(me ^ k, t ^ x, r ^ c) for k in range(owners) for x in (0, 1) for c in (0, 1)][1:]
-    for peer in peers:
-        pl.semaphore_signal(barrier, inc=1, device_id=peer, device_id_type=MESH)
 
     loads[0].wait()
     routing = routing_ref[...]
@@ -220,10 +221,11 @@
         cols[me, r, n] = ((g / (1.0 + jnp.exp(-g))) * u).astype(jnp.bfloat16)
         for k in STEPS:
             to_group(k, n).start()
+        to_core(0, n).start()
+
+    for n in range(pieces):
         for core in (0, 1):
             to_strip(n, core).start()
-        to_core(0, n).start()
-
     count_copy.wait()
     half_mine[...] = 2.0 / jnp.maximum(half_mine[...] + half_other[...], 1.0)
 

time: 25.1 us -> 24.7 us (0.984)
  Pallas kernels: 25 us -> 24.5 us
    pallas_call x1, Pallas kernels: 23 us -> 22.6 us  [fused(): pl.pallas_call(functools.partial(hessian_kernel, owners), out_shape=jax.S...]
where the time goes in v3:
time: 24.7 us; the launch traced here: 24.6 us
  Pallas kernels  24.5 us (99%)
    pallas_call x1, Pallas kernels, fused(): pl.pallas_call(functools.partial(hessian_kernel, owners), out_shape=jax.S...  22.6 us
    pallas_call x1, Pallas kernels, fused(): pl.pallas_call(order_kernel, out_shape=jax.ShapeDtypeStruct(out, jnp.floa...  1.92 us

profile of v3, /device:TPU:1, one launch (start us, length us, event | category | flops | bytes accessed | tf_op | source)
XLA Modules:
  0.0 24.6 jit_solution(3326887497855359605)
XLA Ops:
  0.0 0.0 copy-start
  0.0 22.6 %shard_map.55.hess_ref = f32[4,128,512]{2,1,0:T(8,128)S(1)} custom-call(bf16[128,3584]{1,0:T(8,128)(2,1)} %tokens_hbm.1, s32[8,128]{1,0:T(8,128)} %bitcast.1, bf16[1,3584,512]{2,1,0:T(8,128)(2,1)} %gate_hbm.1, bf16[1,3584,512]{2,1,0:T(8,128)(2,1)} %up_hbm.1), custom_call_target="tpu_custom_call" | custom-call | tf_op jit(solution)/shard_map/pallas_call | solution.py:297
  22.6 0.0 copy-done
  22.6 1.9 %shard_map.56 = f32[8,128,512]{2,1,0:T(8,128)} custom-call(s32[8]{0:T(128)S(1)} %copy-done, f32[4,128,512]{2,1,0:T(8,128)S(1)} %shard_map.55.hess_ref), custom_call_target="tpu_custom_call" | custom-call | tf_op jit(solution)/shard_map/pallas_call | solution.py:326
Async XLA Ops:
  0.0 22.6 %copy-start = (s32[8]{0:T(128)S(1)}, s32[8]{0:T(128)}, u32[]{:S(2)}) copy-start(s32[8]{0:T(128)} %chosen_ref.1) | copy-start | bytes 100

commit v4 on v3

--- a/solution.py
+++ b/solution.py
@@ -195,11 +195,11 @@
     loads[3].wait()
 
     def to_group(k, n):
-        here = cols.at[me, r, n]
+        here = cols.at[me, r]
         return remote(here, here, az_send.at[k, n], az_recv.at[k, n], place(me ^ k, t, r))
 
     def to_core(k, n):
-        here = cols.at[me ^ k, r, n]
+        here = cols.at[me ^ k, r]
         return remote(here, here, ar_send.at[k, n], ar_recv.at[k, n], place(me, t, 1 - r))
 
     strip_width = rows.shape[3]
@@ -219,9 +219,10 @@
         g = jnp.dot(x, gate[:, at], preferred_element_type=jnp.float32)
         u = jnp.dot(x, up[:, at], preferred_element_type=jnp.float32)
         cols[me, r, n] = ((g / (1.0 + jnp.exp(-g))) * u).astype(jnp.bfloat16)
-        for k in STEPS:
-            to_group(k, n).start()
-        to_core(0, n).start()
+        for k in STEPS if n == pieces - 1 else ():
+            to_group(k, 0).start()
+        if n == pieces - 1:
+            to_core(0, 0).start()
 
     for n in range(pieces):
         for core in (0, 1):
@@ -233,8 +234,7 @@
 
     def hessian(k):
         e = me ^ k
-        for n in range(pieces):
-            to_core(k, n).wait_recv()
+        to_core(k, 0).wait_recv()
 
         @pl.when(t == in_panel)
         def _():
@@ -257,8 +257,10 @@
         for k in (1,) + FAR:
             if n == pieces - 1 and k == FAR[0]:
                 hessian(0)
-            to_group(k, n).wait_recv()
-            to_core(k, n).start()
+            if n == pieces - 1:
+                to_group(k, 0).wait_recv()
+            if n == pieces - 1:
+                to_core(k, 0).start()
     for k in (1,) + FAR:
         hessian(k)
 
@@ -269,9 +271,10 @@
         direct(*d).wait_send()
     for n in range(pieces):
         for k in STEPS:
-            to_group(k, n).wait_send()
-        for k in (0,) + STEPS:
-            to_core(k, n).wait_send()
+            if n == 0:
+                to_group(k, 0).wait_send()
+        for k in (0,) + STEPS if n == 0 else ():
+            to_core(k, 0).wait_send()
         for core in (0, 1):
             to_strip(n, core).wait_send()
 

time: 24.7 us -> 24.7 us (level)
  no operation moved by 1% of the time
where the time goes in v4:
time: 24.7 us; the launch traced here: 24.5 us
  Pallas kernels  24.5 us (99%)
    pallas_call x1, Pallas kernels, fused(): pl.pallas_call(functools.partial(hessian_kernel, owners), out_shape=jax.S...  22.6 us
    pallas_call x1, Pallas kernels, fused(): pl.pallas_call(order_kernel, out_shape=jax.ShapeDtypeStruct(out, jnp.floa...  1.92 us

profile of v4, /device:TPU:1, one launch (start us, length us, event | category | flops | bytes accessed | tf_op | source)
XLA Modules:
  0.0 24.5 jit_solution(13385688338460663316)
XLA Ops:
  0.0 0.0 copy-start
  0.0 22.6 %shard_map.55.hess_ref = f32[4,128,512]{2,1,0:T(8,128)S(1)} custom-call(bf16[128,3584]{1,0:T(8,128)(2,1)} %tokens_hbm.1, s32[8,128]{1,0:T(8,128)} %bitcast.1, bf16[1,3584,512]{2,1,0:T(8,128)(2,1)} %gate_hbm.1, bf16[1,3584,512]{2,1,0:T(8,128)(2,1)} %up_hbm.1), custom_call_target="tpu_custom_call" | custom-call | tf_op jit(solution)/shard_map/pallas_call | solution.py:300
  22.6 0.0 copy-done
  22.6 1.9 %shard_map.56 = f32[8,128,512]{2,1,0:T(8,128)} custom-call(s32[8]{0:T(128)S(1)} %copy-done, f32[4,128,512]{2,1,0:T(8,128)S(1)} %shard_map.55.hess_ref), custom_call_target="tpu_custom_call" | custom-call | tf_op jit(solution)/shard_map/pallas_call | solution.py:329
Async XLA Ops:
  0.0 22.6 %copy-start = (s32[8]{0:T(128)S(1)}, s32[8]{0:T(128)}, u32[]{:S(2)}) copy-start(s32[8]{0:T(128)} %chosen_ref.1) | copy-start | bytes 100
